TPU v7x, 32 devices: a whole 2x2x4 slice. The times are simulated.
32 devices in a mesh: pair: 4 (over z), dof: 8 (over y, x, core).
Axes of the slice: x: 2, y: 2, z: 4, core: 2. Of those that a mesh axis runs over, the one named last changes fastest.
Arguments:
- snapshots: float32 [128, 65536], P('pair', 'dof'), may hold values from -600 to 600
Outputs:
- rotated: float32 [128, 65536], P('pair', 'dof')
All inputs are finite; a program needn't handle non-finite values.
Results may differ from a plain program's by a relative error of at most 0.0003.
Values sent between devices are 32-bit elements; how exact they have to be, the bound alone decides.
A program may use at most 64 MiB of HBM per device.

v0:
```python
import jax
import jax.numpy as jnp
from jax import lax
from jax.sharding import PartitionSpec as P

STEPS = 4
SWEEPS = 2
highest = lax.Precision.HIGHEST


def passed_along(block, axis, distance):
    devices = range(lax.axis_size(axis))
    route = [(i - distance, i) for i in devices if i - distance in devices]
    return lax.ppermute(block, axis, route)


def jacobi(gram_matrix):
    pair_order = gram_matrix.shape[0]
    circle_size = pair_order - 1
    index_row = lax.broadcasted_iota(jnp.int32, (pair_order, pair_order), 0)
    index_col = lax.broadcasted_iota(jnp.int32, (pair_order, pair_order), 1)
    identity_mask = index_row == index_col
    upper_side = index_row < index_col
    indices = jnp.arange(pair_order, dtype=jnp.int32)

    def one_round(round_index, carried):
        gram_now, basis = carried
        shifted = (round_index % circle_size).astype(jnp.int32)
        mirror = (2 * shifted - indices + 2 * circle_size) % circle_size
        partner = jnp.where(
            indices == circle_size, shifted, jnp.where(indices == shifted, circle_size, mirror)
        )
        partner_mask = index_col == partner[:, None]
        zeros = jnp.zeros_like(gram_now)
        upper_part = jnp.where(upper_side, gram_now, gram_now.T)
        coupling = jnp.sum(jnp.where(partner_mask, upper_part, zeros), axis=1)
        own_diag = jnp.sum(jnp.where(identity_mask, gram_now, zeros), axis=1)
        other_diag = jnp.sum(jnp.where(partner_mask, own_diag[None, :] + zeros, zeros), axis=1)
        is_lower = indices < partner
        diag_lower = jnp.where(is_lower, own_diag, other_diag)
        diag_upper = jnp.where(is_lower, other_diag, own_diag)
        spread_diag = diag_upper - diag_lower
        orient = jnp.where(spread_diag >= 0, 1.0, -1.0).astype(jnp.float32)
        tangent = (
            orient
            * 2.0
            * coupling
            / (
                jnp.abs(spread_diag)
                + jnp.sqrt(spread_diag * spread_diag + 4.0 * coupling * coupling)
            )
        )
        cosine = 1.0 / jnp.sqrt(1.0 + tangent * tangent)
        sine_part = cosine * tangent
        signed_sine = jnp.where(is_lower, sine_part, -sine_part)
        rotation = jnp.where(
            identity_mask,
            cosine[:, None] + zeros,
            jnp.where(partner_mask, signed_sine[:, None] + zeros, zeros),
        )
        gram_now = jnp.dot(
            jnp.dot(rotation.T, gram_now, precision=highest), rotation, precision=highest
        )
        basis = jnp.dot(basis, rotation, precision=highest)
        return (gram_now, basis)

    start = (gram_matrix, jnp.eye(pair_order, dtype=jnp.float32))
    final_gram, basis = lax.fori_loop(0, SWEEPS * circle_size, one_round, start)
    return basis


def body(snapshots):
    pair_order = snapshots.shape[0]
    half_order = pair_order // 2
    device_place = lax.axis_index("pair")
    final_place = lax.axis_size("pair") - 1
    is_first = device_place == 0
    is_last = device_place == final_place
    pair_rows = snapshots
    for step_index in range(STEPS):
        local_gram = jnp.dot(pair_rows, pair_rows.T, precision=highest)
        gram_matrix = lax.psum(local_gram, "dof")
        turned = jacobi(gram_matrix)
        moved = jnp.dot(turned.T, pair_rows, precision=highest)
        new_top = moved[:half_order]
        new_low = moved[half_order:]
        rising = jnp.where(is_first, new_low, new_top)
        got_rising = passed_along(rising, "pair", 1)
        got_falling = passed_along(new_low, "pair", -1)
        next_top = jnp.where(is_first, new_top, got_rising)
        next_low = jnp.where(is_last, new_top, got_falling)
        pair_rows = jnp.concatenate([next_top, next_low], axis=0)
    return pair_rows


def solution(mesh):
    in_specs = (P("pair", "dof"),)
    out_specs = P("pair", "dof")
    return jax.shard_map(body, mesh=mesh, in_specs=in_specs, out_specs=out_specs, check_vma=False)
```

profile of v0, /device:TPU:0, one launch (start us, length us, event | category | flops | bytes accessed | tf_op | source)
XLA Modules:
  0.0 519.9 jit_solution(5323736316995581943)
XLA Ops:
  2.2 25.5 %psum.28 = f32[32,32]{1,0:T(8,128)S(1)} all-reduce(f32[32,32]{1,0:T(8,128)S(1)} %fusion.185), channel_id=1, replica_groups=mesh['pair'=4,'dof'=8] {'dof'}, use_global_device_ids=true, to_apply=%region_0.0 | all-reduce | flops 1024 | bytes 8192 | tf_op jit(solution)/shard_map/psum | solution.py:82
  27.7 85.2 %while.76 = (s32[]{:T(128)}, f32[32,32]{1,0:T(8,128)S(1)}, f32[32,32]{0,1:T(8,128)S(1)}, s32[]{:T(128)}, s32[]{:T(128)}, /*index=5*/s32[]{:T(128)}, s32[]{:T(128)}) while((s32[]{:T(128)}, f32[32,32]{1,0:T(8,128)S(1)}, f32[32,32]{0,1:T(8,128)S(1)}, s32[]{:T(128)}, s32[]{:T(128)}, /*index=5*/s32[]{:T(128)}, ...), condition=%wide.region_5.6_spmd.clone.clone, body=%wide.region_1.5_spmd.clone.clone.sunk | while | flops 1205001 | bytes 52267 | solution.py:68
  114.8 3.5 collective-permute-start
  118.3 1.3 collective-permute-start.1
  119.6 7.6 %collective-permute-done = f32[16,8192]{1,0:T(8,128)S(1)} collective-permute-done((f32[16,8192]{1,0:T(8,128)}, f32[16,8192]{1,0:T(8,128)S(1)}, u32[]{:S(2)}, u32[]{:S(2)}) %collective-permute-start) | collective-permute-done | bytes 524320 | tf_op jit(solution)/shard_map/ppermute | solution.py:14
  128.0 3.1 collective-permute-done.1
  133.3 24.1 %psum.29 = f32[32,32]{1,0:T(8,128)S(1)} all-reduce(f32[32,32]{1,0:T(8,128)S(1)} %fusion.173), channel_id=1, replica_groups=mesh['pair'=4,'dof'=8] {'dof'}, use_global_device_ids=true, to_apply=%region_6.7 | all-reduce | flops 1024 | bytes 8192 | tf_op jit(solution)/shard_map/psum | solution.py:82
  157.4 85.2 %while.77 = (s32[]{:T(128)}, f32[32,32]{1,0:T(8,128)S(1)}, f32[32,32]{0,1:T(8,128)S(1)}, s32[]{:T(128)}, s32[]{:T(128)}, /*index=5*/s32[]{:T(128)}, s32[]{:T(128)}) while((s32[]{:T(128)}, f32[32,32]{1,0:T(8,128)S(1)}, f32[32,32]{0,1:T(8,128)S(1)}, s32[]{:T(128)}, s32[]{:T(128)}, /*index=5*/s32[]{:T(128)}, ...), condition=%wide.region_11.12_spmd.clone.clone, body=%wide.region_7.11_spmd.clone.clone.sunk | while | flops 1205001 | bytes 52267 | solution.py:68
  244.4 3.6 collective-permute-start.2
  248.1 1.3 collective-permute-start.3
  249.4 7.6 %collective-permute-done.2 = f32[16,8192]{1,0:T(8,128)S(1)} collective-permute-done((f32[16,8192]{1,0:T(8,128)}, f32[16,8192]{1,0:T(8,128)S(1)}, u32[]{:S(2)}, u32[]{:S(2)}) %collective-permute-start.2) | collective-permute-done | bytes 524320 | tf_op jit(solution)/shard_map/ppermute | solution.py:14
  257.8 3.1 collective-permute-done.3
  263.0 24.2 %psum.30 = f32[32,32]{1,0:T(8,128)S(1)} all-reduce(f32[32,32]{1,0:T(8,128)S(1)} %fusion.171), channel_id=1, replica_groups=mesh['pair'=4,'dof'=8] {'dof'}, use_global_device_ids=true, to_apply=%region_12.13 | all-reduce | flops 1024 | bytes 8192 | tf_op jit(solution)/shard_map/psum | solution.py:82
  287.2 85.2 %while.78 = (s32[]{:T(128)}, f32[32,32]{1,0:T(8,128)S(1)}, f32[32,32]{0,1:T(8,128)S(1)}, s32[]{:T(128)}, s32[]{:T(128)}, /*index=5*/s32[]{:T(128)}, s32[]{:T(128)}) while((s32[]{:T(128)}, f32[32,32]{1,0:T(8,128)S(1)}, f32[32,32]{0,1:T(8,128)S(1)}, s32[]{:T(128)}, s32[]{:T(128)}, /*index=5*/s32[]{:T(128)}, ...), condition=%wide.region_17.18_spmd.clone.clone, body=%wide.region_13.17_spmd.clone.clone.sunk | while | flops 1205001 | bytes 52267 | solution.py:68
  374.3 3.6 collective-permute-start.4
  378.0 1.3 collective-permute-start.5
  379.3 7.6 %collective-permute-done.4 = f32[16,8192]{1,0:T(8,128)S(1)} collective-permute-done((f32[16,8192]{1,0:T(8,128)}, f32[16,8192]{1,0:T(8,128)S(1)}, u32[]{:S(2)}, u32[]{:S(2)}) %collective-permute-start.4) | collective-permute-done | bytes 524320 | tf_op jit(solution)/shard_map/ppermute | solution.py:14
  387.7 3.1 collective-permute-done.5
  392.9 24.2 %psum.31 = f32[32,32]{1,0:T(8,128)S(1)} all-reduce(f32[32,32]{1,0:T(8,128)S(1)} %fusion.169), channel_id=1, replica_groups=mesh['pair'=4,'dof'=8] {'dof'}, use_global_device_ids=true, to_apply=%region_18.19 | all-reduce | flops 1024 | bytes 8192 | tf_op jit(solution)/shard_map/psum | solution.py:82
  417.1 85.2 %while.79 = (s32[]{:T(128)}, f32[32,32]{1,0:T(8,128)S(1)}, f32[32,32]{0,1:T(8,128)S(1)}, s32[]{:T(128)}, s32[]{:T(128)}, /*index=5*/s32[]{:T(128)}, s32[]{:T(128)}) while((s32[]{:T(128)}, f32[32,32]{1,0:T(8,128)S(1)}, f32[32,32]{0,1:T(8,128)S(1)}, s32[]{:T(128)}, s32[]{:T(128)}, /*index=5*/s32[]{:T(128)}, ...), condition=%wide.region_23.24_spmd.clone.clone, body=%wide.region_19.23_spmd.clone.clone.sunk | while | flops 1205001 | bytes 52267 | solution.py:68
  503.4 2.6 collective-permute-start.6
  506.1 1.3 collective-permute-start.7
  507.4 7.3 %collective-permute-done.6 = f32[16,8192]{1,0:T(8,128)S(1)} collective-permute-done((f32[16,8192]{1,0:T(8,128)S(1)}, f32[16,8192]{1,0:T(8,128)S(1)}, u32[]{:S(2)}, u32[]{:S(2)}) %collective-permute-start.6) | collective-permute-done | bytes 524320 | tf_op jit(solution)/shard_map/ppermute | solution.py:14
  514.7 4.1 collective-permute-done.7
  (2516 shorter events, 337.1 us)
Async XLA Ops:
  0.0 1.2 copy-start
  0.0 0.6 copy-start.1
  2.2 25.5 %copy-start.3 = (f32[32,32]{0,1:T(8,128)S(1)}, f32[32,32]{0,1:T(8,128)}, u32[]{:S(2)}) copy-start(f32[32,32]{0,1:T(8,128)} %copy-done.1) | copy-start | bytes 12292
  114.8 12.4 %collective-permute-start = (f32[16,8192]{1,0:T(8,128)}, f32[16,8192]{1,0:T(8,128)S(1)}, u32[]{:S(2)}, u32[]{:S(2)}) collective-permute-start(f32[16,8192]{1,0:T(8,128)} %get-tuple-element.955), channel_id=1, source_target_pairs={{0,8},{8,16},{16,24},{1,9},{9,17},{17,25},{2,10},{10,18},{18,26},{... | collective-permute-start | bytes 1572872 | tf_op jit(solution)/shard_map/ppermute | solution.py:14
  118.3 12.9 %collective-permute-start.1 = (f32[16,8192]{1,0:T(8,128)S(1)}, f32[16,8192]{1,0:T(8,128)}, u32[]{:S(2)}, u32[]{:S(2)}) collective-permute-start(f32[16,8192]{1,0:T(8,128)S(1)} %get-tuple-element.956), channel_id=1, source_target_pairs={{8,0},{16,8},{24,16},{9,1},{17,9},{25,17},{10,2},{18,10},{26,18},{... | collective-permute-start | bytes 1572872 | tf_op jit(solution)/shard_map/ppermute | solution.py:14
  127.2 0.8 copy-start.6
  133.3 24.1 %copy-start.4 = (f32[32,32]{0,1:T(8,128)S(1)}, f32[32,32]{0,1:T(8,128)}, u32[]{:S(2)}) copy-start(f32[32,32]{0,1:T(8,128)} %copy-done.1) | copy-start | bytes 12292
  244.4 12.6 %collective-permute-start.2 = (f32[16,8192]{1,0:T(8,128)}, f32[16,8192]{1,0:T(8,128)S(1)}, u32[]{:S(2)}, u32[]{:S(2)}) collective-permute-start(f32[16,8192]{1,0:T(8,128)} %get-tuple-element.951), channel_id=1, source_target_pairs={{0,8},{8,16},{16,24},{1,9},{9,17},{17,25},{2,10},{10,18},{18,26},{... | collective-permute-start | bytes 1572872 | tf_op jit(solution)/shard_map/ppermute | solution.py:14
  248.1 12.9 %collective-permute-start.3 = (f32[16,8192]{1,0:T(8,128)S(1)}, f32[16,8192]{1,0:T(8,128)}, u32[]{:S(2)}, u32[]{:S(2)}) collective-permute-start(f32[16,8192]{1,0:T(8,128)S(1)} %get-tuple-element.952), channel_id=1, source_target_pairs={{8,0},{16,8},{24,16},{9,1},{17,9},{25,17},{10,2},{18,10},{26,18},{... | collective-permute-start | bytes 1572872 | tf_op jit(solution)/shard_map/ppermute | solution.py:14
  257.0 0.8 copy-start.7
  263.0 24.2 %copy-start.5 = (f32[32,32]{0,1:T(8,128)S(1)}, f32[32,32]{0,1:T(8,128)}, u32[]{:S(2)}) copy-start(f32[32,32]{0,1:T(8,128)} %copy-done.1) | copy-start | bytes 12292
  374.3 12.6 %collective-permute-start.4 = (f32[16,8192]{1,0:T(8,128)}, f32[16,8192]{1,0:T(8,128)S(1)}, u32[]{:S(2)}, u32[]{:S(2)}) collective-permute-start(f32[16,8192]{1,0:T(8,128)} %get-tuple-element.947), channel_id=1, source_target_pairs={{0,8},{8,16},{16,24},{1,9},{9,17},{17,25},{2,10},{10,18},{18,26},{... | collective-permute-start | bytes 1572872 | tf_op jit(solution)/shard_map/ppermute | solution.py:14
  378.0 12.9 %collective-permute-start.5 = (f32[16,8192]{1,0:T(8,128)S(1)}, f32[16,8192]{1,0:T(8,128)}, u32[]{:S(2)}, u32[]{:S(2)}) collective-permute-start(f32[16,8192]{1,0:T(8,128)S(1)} %get-tuple-element.948), channel_id=1, source_target_pairs={{8,0},{16,8},{24,16},{9,1},{17,9},{25,17},{10,2},{18,10},{26,18},{... | collective-permute-start | bytes 1572872 | tf_op jit(solution)/shard_map/ppermute | solution.py:14
  386.9 0.8 copy-start.8
  392.9 24.2 %copy-start.2 = (f32[32,32]{0,1:T(8,128)S(1)}, f32[32,32]{0,1:T(8,128)}, u32[]{:S(2)}) copy-start(f32[32,32]{0,1:T(8,128)} %copy-done.1) | copy-start | bytes 12292
  503.4 11.2 %collective-permute-start.6 = (f32[16,8192]{1,0:T(8,128)S(1)}, f32[16,8192]{1,0:T(8,128)S(1)}, u32[]{:S(2)}, u32[]{:S(2)}) collective-permute-start(f32[16,8192]{1,0:T(8,128)S(1)} %get-tuple-element.943), channel_id=1, source_target_pairs={{0,8},{8,16},{16,24},{1,9},{9,17},{17,25},{2,10},{10,18},{18,26},{... | collective-permute-start | bytes 1572872 | tf_op jit(solution)/shard_map/ppermute | solution.py:14
  506.1 12.7 %collective-permute-start.7 = (f32[16,8192]{1,0:T(8,128)S(1)}, f32[16,8192]{1,0:T(8,128)S(1)}, u32[]{:S(2)}, u32[]{:S(2)}) collective-permute-start(f32[16,8192]{1,0:T(8,128)S(1)} %get-tuple-element.944), channel_id=1, source_target_pairs={{8,0},{16,8},{24,16},{9,1},{17,9},{25,17},{10,2},{18,10},{26,18},{... | collective-permute-start | bytes 1572872 | tf_op jit(solution)/shard_map/ppermute | solution.py:14
where the time goes:
time: 521 us; the launch traced here: 520 us
  matrix products  200 us (38%)
  other arithmetic  115 us (22%)
  blocking collectives  97.9 us (19%)
  waiting for transfers between devices  43.7 us (8%)
  loops' own time  22.4 us (4%)
  local copies, waits for them, and re-layouts  22.1 us (4%)
  starting transfers between devices  18.5 us (4%)
    psum x4, blocking collectives, body(): gram_matrix = lax.psum(local_gram, 'dof')  97.9 us
    dot_general x248, matrix products, one_round(): basis = jnp.dot(basis, rotation, precision=highest)  69.6 us
    dot_general x248, matrix products, one_round(): jnp.dot(rotation.T, gram_now, precision=highest)  69.6 us
    dot_general x248, matrix products, one_round(): jnp.dot(jnp.dot(rotation.T, gram_now, precision=highest), rotation, preci...  52.7 us
    reduce_sum x248, other arithmetic, one_round(): jnp.sum(jnp.where(partner_mask, own_diag[None, :] + zeros, zeros), axis=1)  44.4 us
    ppermute x8, waiting for transfers between devices, passed_along(): return lax.ppermute(block, axis, route)  43.7 us
    reduce_sum x248, other arithmetic, one_round(): own_diag = jnp.sum(jnp.where(identity_mask, gram_now, zeros), axis=1)  43.6 us
    another operation x4, loops' own time, jacobi(): final_gram, basis = lax.fori_loop(0, SWEEPS * circle_size, one_round, start)  22.4 us
  transfers between devices with their start and end apart: 8, of which 8 were waited for; matrix products, arithmetic and copies ran while one was open for 0% of the time, Pallas kernels for 0%

commit v1 on v0

--- a/solution.py
+++ b/solution.py
@@ -79,7 +79,11 @@
     pair_rows = snapshots
     for step_index in range(STEPS):
         local_gram = jnp.dot(pair_rows, pair_rows.T, precision=highest)
-        gram_matrix = lax.psum(local_gram, "dof")
+        gram_matrix = local_gram
+        for hop in (1, 2, 4):
+            gram_matrix = gram_matrix + lax.ppermute(
+                gram_matrix, "dof", [(dev, dev ^ hop) for dev in range(8)]
+            )
         turned = jacobi(gram_matrix)
         moved = jnp.dot(turned.T, pair_rows, precision=highest)
         new_top = moved[:half_order]

time: 521 us -> 456 us (0.88)
  blocking collectives: 97.9 us -> 0 us
  waiting for transfers between devices: 43.7 us -> 67.9 us
  starting transfers between devices: 18.5 us -> 33.2 us
    psum x4 -> x0, blocking collectives: 97.9 us -> none  [body(): gram_matrix = lax.psum(local_gram, 'dof')]
    ppermute x0 -> x12, waiting for transfers between devices: none -> 20.6 us  [body(): lax.ppermute(gram_matrix, 'dof', [(dev, dev ^ hop) for dev in range(8)])]
    ppermute x0 -> x12, starting transfers between devices: none -> 14.7 us  [body(): lax.ppermute(gram_matrix, 'dof', [(dev, dev ^ hop) for dev in range(8)])]
  transfers between devices with their start and end apart: 8 -> 20, of which waited for: 8 -> 20; matrix products, arithmetic and copies ran while one was open for 0% -> 0% of each run, Pallas kernels for 0% -> 0%
where the time goes in v1:
time: 456 us
  matrix products  200 us (44%)
  other arithmetic  112 us (25%)
  waiting for transfers between devices  67.9 us (15%)
  starting transfers between devices  33.2 us (7%)
  loops' own time  22.5 us (5%)
  local copies, waits for them, and re-layouts  21.2 us (5%)
    dot_general x248, matrix products, one_round(): basis = jnp.dot(basis, rotation, precision=highest)  69.5 us
    dot_general x248, matrix products, one_round(): jnp.dot(rotation.T, gram_now, precision=highest)  69.5 us
    dot_general x248, matrix products, one_round(): jnp.dot(jnp.dot(rotation.T, gram_now, precision=highest), rotation, preci...  52.7 us
    ppermute x8, waiting for transfers between devices, passed_along(): return lax.ppermute(block, axis, route)  47.3 us
    reduce_sum x248, other arithmetic, one_round(): jnp.sum(jnp.where(partner_mask, own_diag[None, :] + zeros, zeros), axis=1)  44.4 us
    reduce_sum x248, other arithmetic, one_round(): own_diag = jnp.sum(jnp.where(identity_mask, gram_now, zeros), axis=1)  43.6 us
    another operation x4, loops' own time, jacobi(): final_gram, basis = lax.fori_loop(0, SWEEPS * circle_size, one_round, start)  22.5 us
    ppermute x12, waiting for transfers between devices, body(): lax.ppermute(gram_matrix, 'dof', [(dev, dev ^ hop) for dev in range(8)])  20.6 us
  transfers between devices with their start and end apart: 20, of which 20 were waited for; matrix products, arithmetic and copies ran while one was open for 0% of the time, Pallas kernels for 0%

profile of v1, /device:TPU:0, one launch (start us, length us, event | category | flops | bytes accessed | tf_op | source)
XLA Modules:
  0.0 456.1 jit_solution(18372935482287842840)
XLA Ops:
  3.5 2.8 collective-permute-start.1
  8.1 2.1 collective-permute-start.2
  11.9 85.2 %while.76 = (s32[]{:T(128)}, f32[32,32]{1,0:T(8,128)S(1)}, f32[32,32]{0,1:T(8,128)S(1)}, s32[]{:T(128)}, s32[]{:T(128)}, /*index=5*/s32[]{:T(128)}, s32[]{:T(128)}) while((s32[]{:T(128)}, f32[32,32]{1,0:T(8,128)S(1)}, f32[32,32]{0,1:T(8,128)S(1)}, s32[]{:T(128)}, s32[]{:T(128)}, /*index=5*/s32[]{:T(128)}, ...), condition=%wide.region_4.5_spmd.clone.clone, body=%wide.region_0.4_spmd.clone.clone.sunk | while | flops 1205001 | bytes 52267 | solution.py:68
  99.0 4.0 collective-permute-start.3
  104.3 8.2 %collective-permute-done.3 = f32[16,8192]{1,0:T(8,128)S(1)} collective-permute-done((f32[16,8192]{1,0:T(8,128)}, f32[16,8192]{1,0:T(8,128)S(1)}, u32[]{:S(2)}, u32[]{:S(2)}) %collective-permute-start.3) | collective-permute-done | bytes 524320 | tf_op jit(solution)/shard_map/ppermute | solution.py:14
  113.3 3.1 collective-permute-done.4
  121.3 2.2 collective-permute-done.6
  125.0 2.2 collective-permute-done.7
  127.3 85.2 %while.77 = (s32[]{:T(128)}, f32[32,32]{1,0:T(8,128)S(1)}, f32[32,32]{0,1:T(8,128)S(1)}, s32[]{:T(128)}, s32[]{:T(128)}, /*index=5*/s32[]{:T(128)}, s32[]{:T(128)}) while((s32[]{:T(128)}, f32[32,32]{1,0:T(8,128)S(1)}, f32[32,32]{0,1:T(8,128)S(1)}, s32[]{:T(128)}, s32[]{:T(128)}, /*index=5*/s32[]{:T(128)}, ...), condition=%wide.region_9.10_spmd.clone.clone, body=%wide.region_5.9_spmd.clone.clone.sunk | while | flops 1205001 | bytes 52267 | solution.py:68
  213.6 3.6 collective-permute-start.8
  218.6 7.9 %collective-permute-done.8 = f32[16,8192]{1,0:T(8,128)S(1)} collective-permute-done((f32[16,8192]{1,0:T(8,128)S(1)}, f32[16,8192]{1,0:T(8,128)S(1)}, u32[]{:S(2)}, u32[]{:S(2)}) %collective-permute-start.8) | collective-permute-done | bytes 524320 | tf_op jit(solution)/shard_map/ppermute | solution.py:14
  226.4 4.1 collective-permute-done.9
  234.4 2.2 collective-permute-done.11
  238.1 2.2 collective-permute-done.12
  240.4 85.1 %while.78 = (s32[]{:T(128)}, f32[32,32]{1,0:T(8,128)S(1)}, f32[32,32]{0,1:T(8,128)S(1)}, s32[]{:T(128)}, s32[]{:T(128)}, /*index=5*/s32[]{:T(128)}, s32[]{:T(128)}) while((s32[]{:T(128)}, f32[32,32]{1,0:T(8,128)S(1)}, f32[32,32]{0,1:T(8,128)S(1)}, s32[]{:T(128)}, s32[]{:T(128)}, /*index=5*/s32[]{:T(128)}, ...), condition=%wide.region_14.15_spmd.clone.clone, body=%wide.region_10.14_spmd.clone.clone.sunk | while | flops 1205001 | bytes 52267 | solution.py:68
  326.6 3.5 collective-permute-start.13
  331.4 7.9 %collective-permute-done.13 = f32[16,8192]{1,0:T(8,128)S(1)} collective-permute-done((f32[16,8192]{1,0:T(8,128)S(1)}, f32[16,8192]{1,0:T(8,128)S(1)}, u32[]{:S(2)}, u32[]{:S(2)}) %collective-permute-start.13) | collective-permute-done | bytes 524320 | tf_op jit(solution)/shard_map/ppermute | solution.py:14
  339.2 4.1 collective-permute-done.14
  347.2 2.2 collective-permute-done.16
  351.0 2.2 collective-permute-done.17
  353.2 85.2 %while.79 = (s32[]{:T(128)}, f32[32,32]{1,0:T(8,128)S(1)}, f32[32,32]{0,1:T(8,128)S(1)}, s32[]{:T(128)}, s32[]{:T(128)}, /*index=5*/s32[]{:T(128)}, s32[]{:T(128)}) while((s32[]{:T(128)}, f32[32,32]{1,0:T(8,128)S(1)}, f32[32,32]{0,1:T(8,128)S(1)}, s32[]{:T(128)}, s32[]{:T(128)}, /*index=5*/s32[]{:T(128)}, ...), condition=%wide.region_19.20_spmd.clone.clone, body=%wide.region_15.19_spmd.clone.clone.sunk | while | flops 1205001 | bytes 52267 | solution.py:68
  439.5 2.2 collective-permute-start.18
  443.0 7.9 %collective-permute-done.18 = f32[16,8192]{1,0:T(8,128)S(1)} collective-permute-done((f32[16,8192]{1,0:T(8,128)S(1)}, f32[16,8192]{1,0:T(8,128)S(1)}, u32[]{:S(2)}, u32[]{:S(2)}) %collective-permute-start.18) | collective-permute-done | bytes 524320 | tf_op jit(solution)/shard_map/ppermute | solution.py:14
  450.8 4.1 collective-permute-done.19
  (2544 shorter events, 354.5 us)
Async XLA Ops:
  0.0 1.2 copy-start
  2.2 1.4 collective-permute-start
  3.5 4.5 collective-permute-start.1
  8.1 3.8 collective-permute-start.2
  99.0 13.5 %collective-permute-start.3 = (f32[16,8192]{1,0:T(8,128)}, f32[16,8192]{1,0:T(8,128)S(1)}, u32[]{:S(2)}, u32[]{:S(2)}) collective-permute-start(f32[16,8192]{1,0:T(8,128)} %get-tuple-element.955), channel_id=1, source_target_pairs={{0,8},{8,16},{16,24},{1,9},{9,17},{17,25},{2,10},{10,18},{18,26},{... | collective-permute-start | bytes 1572872 | tf_op jit(solution)/shard_map/ppermute | solution.py:14
  103.0 13.4 %collective-permute-start.4 = (f32[16,8192]{1,0:T(8,128)S(1)}, f32[16,8192]{1,0:T(8,128)}, u32[]{:S(2)}, u32[]{:S(2)}) collective-permute-start(f32[16,8192]{1,0:T(8,128)S(1)} %get-tuple-element.956), channel_id=1, source_target_pairs={{8,0},{16,8},{24,16},{9,1},{17,9},{25,17},{10,2},{18,10},{26,18},{... | collective-permute-start | bytes 1572872 | tf_op jit(solution)/shard_map/ppermute | solution.py:14
  118.5 1.2 collective-permute-start.5
  119.8 3.7 collective-permute-start.6
  123.5 3.7 collective-permute-start.7
  125.0 2.2 copy-start.4
  213.6 12.8 %collective-permute-start.8 = (f32[16,8192]{1,0:T(8,128)S(1)}, f32[16,8192]{1,0:T(8,128)S(1)}, u32[]{:S(2)}, u32[]{:S(2)}) collective-permute-start(f32[16,8192]{1,0:T(8,128)S(1)} %get-tuple-element.951), channel_id=1, source_target_pairs={{0,8},{8,16},{16,24},{1,9},{9,17},{17,25},{2,10},{10,18},{18,26},{... | collective-permute-start | bytes 1572872 | tf_op jit(solution)/shard_map/ppermute | solution.py:14
  217.3 13.3 %collective-permute-start.9 = (f32[16,8192]{1,0:T(8,128)S(1)}, f32[16,8192]{1,0:T(8,128)S(1)}, u32[]{:S(2)}, u32[]{:S(2)}) collective-permute-start(f32[16,8192]{1,0:T(8,128)S(1)} %get-tuple-element.952), channel_id=1, source_target_pairs={{8,0},{16,8},{24,16},{9,1},{17,9},{25,17},{10,2},{18,10},{26,18},{... | collective-permute-start | bytes 1572872 | tf_op jit(solution)/shard_map/ppermute | solution.py:14
  231.6 1.2 collective-permute-start.10
  232.9 3.7 collective-permute-start.11
  236.6 3.7 collective-permute-start.12
  238.1 2.2 copy-start.5
  326.6 12.7 %collective-permute-start.13 = (f32[16,8192]{1,0:T(8,128)S(1)}, f32[16,8192]{1,0:T(8,128)S(1)}, u32[]{:S(2)}, u32[]{:S(2)}) collective-permute-start(f32[16,8192]{1,0:T(8,128)S(1)} %get-tuple-element.947), channel_id=1, source_target_pairs={{0,8},{8,16},{16,24},{1,9},{9,17},{17,25},{2,10},{10,18},{18,26},{... | collective-permute-start | bytes 1572872 | tf_op jit(solution)/shard_map/ppermute | solution.py:14
  330.1 13.3 %collective-permute-start.14 = (f32[16,8192]{1,0:T(8,128)S(1)}, f32[16,8192]{1,0:T(8,128)S(1)}, u32[]{:S(2)}, u32[]{:S(2)}) collective-permute-start(f32[16,8192]{1,0:T(8,128)S(1)} %get-tuple-element.948), channel_id=1, source_target_pairs={{8,0},{16,8},{24,16},{9,1},{17,9},{25,17},{10,2},{18,10},{26,18},{... | collective-permute-start | bytes 1572872 | tf_op jit(solution)/shard_map/ppermute | solution.py:14
  344.4 1.2 collective-permute-start.15
  345.7 3.7 collective-permute-start.16
  349.4 3.7 collective-permute-start.17
  351.0 2.2 copy-start.2
  439.5 11.4 %collective-permute-start.18 = (f32[16,8192]{1,0:T(8,128)S(1)}, f32[16,8192]{1,0:T(8,128)S(1)}, u32[]{:S(2)}, u32[]{:S(2)}) collective-permute-start(f32[16,8192]{1,0:T(8,128)S(1)} %get-tuple-element.943), channel_id=1, source_target_pairs={{0,8},{8,16},{16,24},{1,9},{9,17},{17,25},{2,10},{10,18},{18,26},{... | collective-permute-start | bytes 1572872 | tf_op jit(solution)/shard_map/ppermute | solution.py:14
  441.7 13.3 %collective-permute-start.19 = (f32[16,8192]{1,0:T(8,128)S(1)}, f32[16,8192]{1,0:T(8,128)S(1)}, u32[]{:S(2)}, u32[]{:S(2)}) collective-permute-start(f32[16,8192]{1,0:T(8,128)S(1)} %get-tuple-element.944), channel_id=1, source_target_pairs={{8,0},{16,8},{24,16},{9,1},{17,9},{25,17},{10,2},{18,10},{26,18},{... | collective-permute-start | bytes 1572872 | tf_op jit(solution)/shard_map/ppermute | solution.py:14
  (3 other events, 2.5 us)
